TPU v7x, 256 devices: a whole 4x4x8 slice. The times are simulated.
256 devices in a mesh: dp: 2 (over core), ctx: 16 (over z, x_lo), tp: 8 (over y, x_hi).
Axes of the slice: x: 4 (x_hi: 2, x_lo: 2; x = x_hi * 2 + x_lo), y: 4, z: 8, core: 2. Of those that a mesh axis runs over, the one named last changes fastest.
Arguments:
- queries: bfloat16 [2, 8192, 4096], P('dp', 'ctx', 'tp'), may hold values from -6 to 6
- keys: bfloat16 [2, 8192, 1024], P('dp', 'ctx', 'tp'), may hold values from -6 to 6
- values: bfloat16 [2, 8192, 1024], P('dp', 'ctx', 'tp'), may hold values from -6 to 6
- document_lengths: int32 [2, 16], P('dp'), may hold values from 1 to 4096, 8192 in all within a row
- out_weight: bfloat16 [4096, 5120], P('tp', 'dp'), may hold values from -0.09375 to 0.09375
Outputs:
- projected: bfloat16 [2, 8192, 5120], P('dp', 'ctx', 'tp')
Inputs may be any that keep to these rules, and one draw needn't show every extreme that they name: `document_lengths`: each row sums to 8192; its largest entry is exactly 4096.
All inputs are finite; a program needn't handle non-finite values.
Results may differ from a plain program's by a relative error of at most 0.015.
Values may be sent and summed in bfloat16 or wider, within the bound.
A program may use at most 64 MiB of HBM per device.

v0:
```python
import math

import jax
import jax.numpy as jnp
from jax import lax
from jax.sharding import PartitionSpec as P

HEAD_SIZE = 128


def document_of(positions, doc_ends):
    return jnp.sum((positions[:, None] >= doc_ends[None, :]).astype(jnp.int32), axis=1)


def shards(queries, keys, values, document_lengths, out_weight):
    block_rows = queries.shape[1]
    query_heads = queries.shape[2] // HEAD_SIZE
    kv_heads = keys.shape[2] // HEAD_SIZE
    heads_per_group = query_heads // kv_heads
    score_scale = HEAD_SIZE ** (-0.5)
    doc_ends = jnp.cumsum(document_lengths[0])
    ctx_index = lax.axis_index("ctx")
    query_first = ctx_index * block_rows
    query_pos = query_first + jnp.arange(block_rows, dtype=jnp.int32)
    query_docs = document_of(query_pos, doc_ends)
    query_tensor = queries[0].reshape(block_rows, kv_heads, heads_per_group, HEAD_SIZE)

    def tile_update(state, key_tile, value_tile, key_first):
        width = key_tile.shape[0]
        key_pos = key_first + jnp.arange(width, dtype=jnp.int32)
        key_docs = document_of(key_pos, doc_ends)
        allowed = (
            (key_pos[None, :] <= query_pos[:, None])
            & (key_docs[None, :] == query_docs[:, None])
            & (key_pos[None, :] >= 0)
        )
        key_tensor = key_tile.reshape(width, kv_heads, HEAD_SIZE)
        value_tensor = value_tile.reshape(width, kv_heads, HEAD_SIZE)
        scores = (
            jnp.einsum(
                "qhgd,khd->hgqk", query_tensor, key_tensor, preferred_element_type=jnp.float32
            )
            * score_scale
        )
        peak_old, total_old, accum_old = state
        peak_new = jnp.maximum(peak_old, jnp.max(jnp.where(allowed, scores, -1e30), axis=-1))
        weights = jnp.where(allowed, jnp.exp(scores - peak_new[..., None]), 0.0)
        factor = jnp.exp(peak_old - peak_new)
        total_new = total_old * factor + jnp.sum(weights, axis=-1)
        accum_new = accum_old * factor[..., None] + jnp.einsum(
            "hgqk,khd->hgqd",
            weights.astype(jnp.bfloat16),
            value_tensor,
            preferred_element_type=jnp.float32,
        )
        return (peak_new, total_new, accum_new)

    initial = (
        jnp.full((kv_heads, heads_per_group, block_rows), -1e30, jnp.float32),
        jnp.zeros((kv_heads, heads_per_group, block_rows), jnp.float32),
        jnp.zeros((kv_heads, heads_per_group, block_rows, HEAD_SIZE), jnp.float32),
    )
    key_piece = lax.all_gather(keys[0], "ctx", axis=0, tiled=True)
    value_piece = lax.all_gather(values[0], "ctx", axis=0, tiled=True)
    count = key_piece.shape[0]
    sub_rows = math.gcd(count, 512)
    tile_count = count // sub_rows
    stacked_keys = key_piece.reshape(tile_count, sub_rows, key_piece.shape[1])
    stacked_values = value_piece.reshape(tile_count, sub_rows, value_piece.shape[1])
    offsets = jnp.arange(tile_count, dtype=jnp.int32) * sub_rows

    def scan_step(inner, inputs):
        key_tile, value_tile, offset = inputs
        return (tile_update(inner, key_tile, value_tile, offset), None)

    final_state, unused = lax.scan(scan_step, initial, (stacked_keys, stacked_values, offsets))
    state = final_state
    peak_final, total_final, accum_final = state
    attended = jnp.transpose(accum_final / total_final[..., None], (2, 0, 1, 3))
    attended = attended.reshape(block_rows, query_heads * HEAD_SIZE).astype(jnp.bfloat16)
    partial_terms = jnp.dot(
        attended,
        lax.all_gather(out_weight, "dp", axis=1, tiled=True),
        preferred_element_type=jnp.float32,
    )[None]
    summed = lax.psum_scatter(
        partial_terms.astype(jnp.bfloat16), "tp", scatter_dimension=2, tiled=True
    )
    return summed


def solution(mesh):
    in_specs = (
        P("dp", "ctx", "tp"),
        P("dp", "ctx", "tp"),
        P("dp", "ctx", "tp"),
        P("dp", None),
        P("tp", "dp"),
    )
    out_specs = P("dp", "ctx", "tp")
    return jax.shard_map(shards, mesh=mesh, in_specs=in_specs, out_specs=out_specs, check_vma=False)
```

profile of v0, /device:TPU:96, one launch (start us, length us, event | category | flops | bytes accessed | tf_op | source)
XLA Modules:
  0.0 474.8 jit_solution(17532140879627081066)
XLA Ops:
  11.4 70.9 %all-gather.8.cloned.1.call-done = bf16[1,8192,128]{2,1,0:T(8,128)(2,1)} async-done(((bf16[1,512,128]{2,1,0:T(8,128)(2,1)}), bf16[1,8192,128]{2,1,0:T(8,128)(2,1)}) %all-gather.8.cloned.1.call-update) | async-done | bytes 2097168 | tf_op jit(solution)/shard_map/all_gather | solution.py:63
  82.2 72.9 %all-gather.10.cloned.1.call-done = bf16[1,8192,128]{2,1,0:T(8,128)(2,1)} async-done(((bf16[1,512,128]{2,1,0:T(8,128)(2,1)}), bf16[1,8192,128]{2,1,0:T(8,128)(2,1)}) %all-gather.10.cloned.1.call-update) | async-done | bytes 2097168 | tf_op jit(solution)/shard_map/all_gather | solution.py:64
  155.1 175.6 %while.15 = (s32[]{:T(128)}, f32[1,4,512]{2,1,0:T(4,128)S(1)}, f32[1,4,512]{2,1,0:T(4,128)S(1)}, f32[1,4,512,128]{3,2,1,0:T(8,128)S(1)}, s32[16]{0:T(128)S(1)}, ...) while((s32[]{:T(128)}, f32[1,4,512]{2,1,0:T(4,128)S(1)}, ...), condition=%wide.region_6.7_spmd.clone, body=%wide.region_2.6_spmd.clone.sunk | while | flops 550278656 | bytes 33442044 | solution.py:76
  161.2 3.8 fusion.42
  168.3 4.0 fusion.39
  172.3 4.6 fusion.42
  184.0 3.8 fusion.42
  194.9 3.8 fusion.42
  205.8 3.8 fusion.42
  216.7 3.8 fusion.42
  227.7 3.8 fusion.42
  238.6 3.8 fusion.42
  249.5 3.8 fusion.42
  260.4 3.8 fusion.42
  271.3 3.8 fusion.42
  282.2 3.8 fusion.42
  293.1 3.8 fusion.42
  304.1 3.8 fusion.42
  315.0 3.8 fusion.42
  325.9 3.8 fusion.42
  331.2 7.1 %fusion.28 = bf16[1,512,5120]{2,1,0:T(8,128)(2,1)} fusion(bf16[512,512]{0,1:T(8,128)(2,1)S(1)} %bitcast.104, bf16[512,5120]{1,0:T(8,128)(2,1)} %all-gather.6.cloned.1.call-done), kind=kOutput, calls=%fused_computation.35 | convolution fusion | flops 2686976000 | bytes 11010048 | tf_op jit(solution)/shard_map/dot_general | solution.py:81
  338.3 21.8 %copy.24 = bf16[1,512,5120]{1,0,2:T(2,128)(2,1)} copy(bf16[1,512,5120]{2,1,0:T(8,128)(2,1)} %fusion.28) | data formatting | bytes 10485760
  360.1 7.9 %copy.28 = bf16[5120,1,512]{2,0,1:T(8,128)(2,1)} copy(bf16[5120,1,512]{2,1,0:T(2,128)(2,1)} %bitcast.99) | data formatting | bytes 10485760
  368.0 96.0 %reduce-scatter.4.cloned.1.call-done = bf16[640,512]{1,0:T(8,128)(2,1)} async-done(((bf16[5120,512]{1,0:T(8,128)(2,1)}), bf16[640,512]{1,0:T(8,128)(2,1)}) %reduce-scatter.4.cloned.1.call-update) | async-done | bytes 655376
  (215 shorter events, 117.9 us)
Async XLA Ops:
  6.5 75.7 %all-gather.8.cloned.1.call-start = ((), (), s32[]{:S(2)}) async-start(), calls=%async_computation.2 | async-start | bytes 2228224 | tf_op jit(solution)/shard_map/all_gather | solution.py:63
  7.3 147.8 %all-gather.10.cloned.1.call-start = ((), (), s32[]{:S(2)}) async-start(), calls=%async_computation.3 | async-start | bytes 2228224 | tf_op jit(solution)/shard_map/all_gather | solution.py:64
  8.0 323.2 %all-gather.6.cloned.1.call-start = ((), (), s32[]{:S(2)}) async-start(), calls=%async_computation.1 | async-start | bytes 7864320 | tf_op jit(solution)/shard_map/all_gather | solution.py:83
  8.7 455.2 %reduce-scatter.4.cloned.1.call-start = ((), (), s32[]{:S(2)}) async-start(), calls=%async_computation.4 | async-start | bytes 5898240
  161.2 3.9 copy-start
  172.3 4.7 copy-start
  184.0 3.9 copy-start
  194.9 3.9 copy-start
  205.8 3.9 copy-start
  216.7 3.9 copy-start
  227.6 3.9 copy-start
  238.6 3.9 copy-start
  249.5 3.9 copy-start
  260.4 3.9 copy-start
  271.3 3.9 copy-start
  282.2 3.9 copy-start
  293.1 3.9 copy-start
  304.0 3.9 copy-start
  315.0 3.9 copy-start
  325.9 3.9 copy-start
Sparse Core Ops, SparseCore 0:
  9.1 73.0 all-gather.7
  84.0 71.0 all-gather.9
  156.9 20.4 all-gather.5
  368.1 95.8 reduce-scatter.3
where the time goes:
time: 477 us; the launch traced here: 475 us
  waiting for transfers between devices  242 us (51%)
  matrix products  130 us (27%)
  local copies, waits for them, and re-layouts  46.5 us (10%)
  other arithmetic  42.2 us (9%)
  between operations  13.2 us (3%)
    unnamed x5, waiting for transfers between devices  98.1 us
    all_gather x1, waiting for transfers between devices, shards(): value_piece = lax.all_gather(values[0], 'ctx', axis=0, tiled=True)  72.9 us
    all_gather x1, waiting for transfers between devices, shards(): key_piece = lax.all_gather(keys[0], 'ctx', axis=0, tiled=True)  70.9 us
    dot_general x16, matrix products, tile_update(): jnp.einsum('hgqk,khd->hgqd', weights.astype(jnp.bfloat16), value_tensor,...  62.2 us
    dot_general x16, matrix products, tile_update(): jnp.einsum('qhgd,khd->hgqk', query_tensor, key_tensor, preferred_element_...  60.6 us
    unnamed x6, local copies, waits for them, and re-layouts  35.5 us
    reduce_sum x16, other arithmetic, tile_update(): total_new = total_old * factor + jnp.sum(weights, axis=-1)  14.6 us
    ge x16, other arithmetic, tile_update(): key_pos[None, :] >= 0  10.2 us
  transfers between devices with their start and end apart: 4, of which 3 were waited for; matrix products, arithmetic and copies ran while one was open for 37% of the time, Pallas kernels for 0%

commit v1 on v0

v1 whole, which is shorter than its diff:
```python
import functools

import jax
import jax.numpy as jnp
from jax import lax
from jax.experimental import pallas as pl
from jax.experimental.pallas import tpu as pltpu
from jax.sharding import PartitionSpec as P

HEAD = 128
LOG2E = 1.4426950408889634
APART = 16384.0
MESH = pl.DeviceIdType.MESH


def kernel(
    shape, q_hbm, k_hbm, v_hbm, lens, w_hbm, out_hbm,
    qv, kc, vc, qd, qc, sc, mx, acc, att, wb, mine, give, take, outv,
    loc_sem, zs, zr, xs, xr, ws, wr, fs, fr, ags, agr, fws, fwr, rss, rsr, outs,
):
    ncore, nctx, ntp, rows, heads, chunk = shape
    nchunk = rows // chunk
    half = chunk // 2
    stacked = heads * chunk
    cols = wb.shape[2] // 2
    slots = kc.shape[0]
    hops = (slots - 1) // 2
    ny = ntp // 2

    core, ctx, tp = lax.axis_index("dp"), lax.axis_index("ctx"), lax.axis_index("tp")
    lo = ctx % 2
    y, hi = tp // 2, tp % 2
    up = (core, (ctx + 2) % nctx, tp)
    down = (core, (ctx + nctx - 2) % nctx, tp)
    pair = (core, ctx + 1 - 2 * lo, tp)
    yp = (core, ctx, (tp + 2) % ntp)
    ym = (core, ctx, (tp + ntp - 2) % ntp)
    yo = (core, ctx, (tp + 4) % ntp)
    mate = (core, ctx, tp + 1 - 2 * hi)
    twin = (1 - core, ctx, tp)

    barrier = pltpu.get_barrier_semaphore()
    peers = (up, down, pair, yp, ym, yo, mate, twin)
    for peer in peers:
        pl.semaphore_signal(barrier, inc=1, device_id=peer, device_id_type=MESH)
    pl.semaphore_wait(barrier, len(peers))

    def remote(src, dst, send, recv, dev):
        return pltpu.make_async_remote_copy(
            src_ref=src, dst_ref=dst, send_sem=send, recv_sem=recv, device_id=dev, device_id_type=MESH
        )

    bank = (kc, vc)
    inputs = (k_hbm, v_hbm)

    def z_copy(j, p, src=None):
        src = bank[p].at[2 * j - 2, :, 0:HEAD] if src is None else src
        return remote(src, bank[p].at[2 * j, :, 0:HEAD], zs.at[j - 1, p], zr.at[j - 1, p], up)

    def x_copy(i, p, src=None):
        src = bank[p].at[2 * i + 2 * lo, :, 0:HEAD] if src is None else src
        return remote(src, bank[p].at[2 * i + 1, :, 0:HEAD], xs.at[i, p], xr.at[i, p], pair)

    for p in range(2):
        z_copy(1, p, inputs[p].at[0]).start()

        @pl.when(lo == 0)
        def _():
            x_copy(0, p, inputs[p].at[0]).start()

    own = [pltpu.make_async_copy(inputs[p].at[0], bank[p].at[0, :, 0:HEAD], loc_sem.at[p]) for p in range(2)]
    own.append(pltpu.make_async_copy(q_hbm.at[0], qv, loc_sem.at[2]))
    for c in own:
        c.start()

    has_cols = (y // 2) == core

    def w_copy(i, dst_tp):
        return remote(w_hbm.at[:, pl.ds(i * 2 * cols, 2 * cols)], wb.at[y], ws.at[i], wr.at[y], (core, ctx, dst_tp))

    def w_here(i):
        return pltpu.make_async_copy(w_hbm.at[:, pl.ds(i * 2 * cols, 2 * cols)], wb.at[y], loc_sem.at[3])

    for i in range(2):
        dst_y = 2 * core + i

        @pl.when(dst_y != y)
        def _():
            w_copy(i, dst_y * 2 + hi).start()

        @pl.when(dst_y == y)
        def _():
            w_here(i).start()

    lane = lax.broadcasted_iota(jnp.int32, (1, HEAD), 1)
    ends = jnp.zeros((1, HEAD), jnp.int32)
    starts = jnp.zeros((1, HEAD), jnp.int32)
    for j in range(lens.shape[1]):
        ends = ends + jnp.where(lane >= j, lens[0, j], 0)
        starts = starts + jnp.where(lane > j, lens[0, j], 0)
    ends = jnp.where(lane < lens.shape[1], ends, 0)

    def in_doc(first):
        pos = first + lax.broadcasted_iota(jnp.int32, (rows, HEAD), 0)
        return (pos >= starts) & (pos < ends)

    qd[...] = jnp.where(in_doc(ctx * rows), APART, 0.0).astype(jnp.bfloat16)

    def mark(d, carry):
        kc[d, :, HEAD:] = jnp.where(in_doc((ctx - d) * rows), 0.0, -1.0).astype(jnp.bfloat16)
        vc[d, :, HEAD:] = jnp.ones((rows, HEAD), jnp.bfloat16)
        return carry

    lax.fori_loop(0, slots, mark, 0)

    for j in range(1, hops + 1):
        for p in range(2):
            z_copy(j, p).wait_recv()
            if j < hops:
                z_copy(j + 1, p).start()
                x_copy(j - lo, p).start()
            else:

                @pl.when(lo == 1)
                def _():
                    x_copy(hops - 1, p).start()

    for c in own:
        c.wait()
    for i in range(hops):
        for p in range(2):
            x_copy(i, p).wait_recv()

    scale = LOG2E * HEAD ** (-0.5)
    dims = (((1,), (1,)), ((), ()))

    def scores(d):
        return lax.dot_general(qc[...], kc[d], dims, preferred_element_type=jnp.float32)

    def lane_max(s):
        m = s[:, 0:HEAD]
        for g in range(1, rows // HEAD):
            m = jnp.maximum(m, s[:, g * HEAD : (g + 1) * HEAD])
        return m

    def attend(c):
        first = pl.multiple_of(c * chunk, chunk)
        for h in range(heads):
            qc[h * chunk : (h + 1) * chunk, 0:HEAD] = qv[pl.ds(first, chunk), h * HEAD : (h + 1) * HEAD]
            qc[h * chunk : (h + 1) * chunk, HEAD:] = qd[pl.ds(first, chunk), :]
        s = scores(0)
        row = lax.broadcasted_iota(jnp.int32, (stacked, rows), 0) % chunk + first
        col = lax.broadcasted_iota(jnp.int32, (stacked, rows), 1)
        s = jnp.where(col <= row, s, -1e30)
        sc[0] = s
        mx[...] = lane_max(s)

        def score_step(d, carry):
            t = scores(d)
            sc[d] = t
            mx[...] = jnp.maximum(mx[...], lane_max(t))
            return carry

        lax.fori_loop(1, slots, score_step, 0)
        peak = jnp.max(mx[...], axis=1, keepdims=True) * scale
        mx[...] = jnp.broadcast_to(peak, mx.shape)
        acc[...] = jnp.zeros_like(acc)

        def value_step(d, carry):
            top = mx[:, 0:1]
            w16 = jnp.exp2(sc[d] * scale - top).astype(jnp.bfloat16)
            acc[...] += jnp.dot(w16, vc[d], preferred_element_type=jnp.float32)
            return carry

        lax.fori_loop(0, slots, value_step, 0)
        for h in range(heads):
            part = acc[h * chunk : (h + 1) * chunk, 0:HEAD] / acc[h * chunk : (h + 1) * chunk, HEAD:]
            att[y, pl.ds(first, chunk), h * HEAD : (h + 1) * HEAD] = part.astype(jnp.bfloat16)

    def at_y(k):
        return lax.rem(y + k, ny)

    def spread(c, way):
        rng = pl.ds(pl.multiple_of(c * chunk, chunk), chunk)
        ref = att.at[y, rng]
        return remote(ref, ref, ags.at[way, c], agr.at[way, c], (yp, ym)[way])

    def spread_in(c, way):
        rng = pl.ds(pl.multiple_of(c * chunk, chunk), chunk)
        ref = att.at[at_y(ny - 1 if way == 0 else 1), rng]
        return remote(ref, ref, ags.at[way, c], agr.at[way, c], (yp, ym)[way])

    def pass_on(c, way):
        rng = pl.ds(pl.multiple_of(c * chunk + way * half, half), half)
        ref = att.at[at_y(ny - 1 if way == 0 else 1), rng]
        return remote(ref, ref, fws.at[way, c], fwr.at[way, c], (yp, ym)[way])

    def pass_in(c, way):
        rng = pl.ds(pl.multiple_of(c * chunk + way * half, half), half)
        ref = att.at[at_y(2), rng]
        return remote(ref, ref, fws.at[way, c], fwr.at[way, c], (yp, ym)[way])

    def swap(c):
        rng = pl.ds(pl.multiple_of(c * chunk, chunk), chunk)
        return remote(give.at[rng], take.at[rng], rss.at[c], rsr.at[c], mate)

    def to_out(c):
        rng = pl.ds(pl.multiple_of(c * chunk, chunk), chunk)
        return pltpu.make_async_copy(outv.at[rng], out_hbm.at[0, rng], outs.at[c])

    def w_share(g):
        return remote(wb.at[g], wb.at[g], fs.at[g], fr.at[g], twin)

    def product(c, side):
        rng = pl.ds(pl.multiple_of(c * chunk, chunk), chunk)
        first = pl.multiple_of(side * cols, HEAD)
        total = jnp.dot(att[0, rng, :], wb[0, :, pl.ds(first, cols)], preferred_element_type=jnp.float32)
        for g in range(1, ny):
            total += jnp.dot(att[g, rng, :], wb[g, :, pl.ds(first, cols)], preferred_element_type=jnp.float32)
        return total

    def step(it, carry):
        @pl.when(it < nchunk)
        def _():
            attend(it)
            for way in range(2):
                spread(it, way).start()

        @pl.when((it == 0) & has_cols)
        def _():
            for i in range(2):

                @pl.when(2 * core + i == y)
                def _():
                    w_here(i).wait()

            w_share(y).start()
            for k in range(1, ny):
                g = at_y(k)
                remote(wb.at[g], wb.at[g], ws.at[0], wr.at[g], yp).wait_recv()
                w_share(g).start()

        @pl.when((it >= 1) & (it <= nchunk))
        def _():
            for way in range(2):
                spread_in(it - 1, way).wait_recv()
                pass_on(it - 1, way).start()

        @pl.when((it == 2) & jnp.logical_not(has_cols))
        def _():
            for g in range(ny):
                w_share(g).wait_recv()

        @pl.when((it >= 2) & (it <= nchunk + 1))
        def _():
            c = it - 2
            rng = pl.ds(pl.multiple_of(c * chunk, chunk), chunk)
            for way in range(2):
                pass_in(c, way).wait_recv()
            give[rng, :] = product(c, 1 - hi).astype(jnp.bfloat16)
            swap(c).start()
            mine[rng, :] = product(c, hi)

        @pl.when(it >= 3)
        def _():
            c = it - 3
            rng = pl.ds(pl.multiple_of(c * chunk, chunk), chunk)
            swap(c).wait_recv()
            outv[rng, :] = (mine[rng, :] + take[rng, :].astype(jnp.float32)).astype(jnp.bfloat16)
            to_out(c).start()

        return carry

    lax.fori_loop(0, nchunk + 3, step, 0)

    for j in range(1, hops + 1):
        for p in range(2):
            z_copy(j, p).wait_send()
            x_copy(j - 1, p).wait_send()
    for i in range(2):

        @pl.when(2 * core + i != y)
        def _():
            w_copy(i, tp).wait_send()

    @pl.when(has_cols)
    def _():
        for g in range(ny):
            w_share(g).wait_send()

    def drain(c, carry):
        for way in range(2):
            spread(c, way).wait_send()
            pass_on(c, way).wait_send()
        swap(c).wait_send()
        to_out(c).wait()
        return carry

    lax.fori_loop(0, nchunk, drain, 0)


def shards(ncore, nctx, ntp, queries, keys, values, document_lengths, out_weight):
    rows = queries.shape[1]
    heads = queries.shape[2] // keys.shape[2]
    depth = out_weight.shape[0]
    cols = out_weight.shape[1] * ncore // ntp
    chunk = 128
    nchunk = rows // chunk
    hops = 4
    slots = 2 * hops + 1
    ny = ntp // 2
    bf16, f32 = jnp.bfloat16, jnp.float32
    dma = pltpu.SemaphoreType.DMA
    any_spec = pl.BlockSpec(memory_space=pl.ANY)
    return pl.pallas_call(
        functools.partial(kernel, (ncore, nctx, ntp, rows, heads, chunk)),
        out_shape=jax.ShapeDtypeStruct((1, rows, cols), bf16),
        in_specs=[any_spec, any_spec, any_spec, pl.BlockSpec(memory_space=pltpu.SMEM), any_spec],
        out_specs=any_spec,
        scratch_shapes=[
            pltpu.VMEM((rows, heads * HEAD), bf16),
            pltpu.VMEM((slots, rows, 2 * HEAD), bf16),
            pltpu.VMEM((slots, rows, 2 * HEAD), bf16),
            pltpu.VMEM((rows, HEAD), bf16),
            pltpu.VMEM((heads * chunk, 2 * HEAD), bf16),
            pltpu.VMEM((slots, heads * chunk, rows), f32),
            pltpu.VMEM((heads * chunk, HEAD), f32),
            pltpu.VMEM((heads * chunk, 2 * HEAD), f32),
            pltpu.VMEM((ny, rows, heads * HEAD), bf16),
            pltpu.VMEM((ny, depth, 2 * cols), bf16),
            pltpu.VMEM((rows, cols), f32),
            pltpu.VMEM((rows, cols), bf16),
            pltpu.VMEM((rows, cols), bf16),
            pltpu.VMEM((rows, cols), bf16),
            dma((4,)),
            dma((hops, 2)), dma((hops, 2)), dma((hops, 2)), dma((hops, 2)),
            dma((2,)), dma((ny,)), dma((ny,)), dma((ny,)),
            dma((2, nchunk)), dma((2, nchunk)), dma((2, nchunk)), dma((2, nchunk)),
            dma((nchunk,)), dma((nchunk,)), dma((nchunk,)),
        ],
        compiler_params=pltpu.CompilerParams(
            collective_id=0, has_side_effects=True, vmem_limit_bytes=56 * 1024 * 1024
        ),
        name="attend_project",
    )(queries, keys, values, document_lengths, out_weight)


def solution(mesh):
    sizes = (mesh.shape["dp"], mesh.shape["ctx"], mesh.shape["tp"])
    in_specs = (P("dp", "ctx", "tp"), P("dp", "ctx", "tp"), P("dp", "ctx", "tp"), P("dp", None), P("tp", "dp"))
    return jax.shard_map(
        functools.partial(shards, *sizes), mesh=mesh, in_specs=in_specs, out_specs=P("dp", "ctx", "tp"), check_vma=False
    )
```

time: 477 us -> 83.5 us (0.18)
  the two profiles are of different devices: /device:TPU:96 before, /device:TPU:8 now
where the time goes in v1:
time: 83.5 us; the launch traced here: 83.4 us
  Pallas kernels  81.4 us (97%)
  local copies, waits for them, and re-layouts  1.98 us (2%)
    pallas_call x1, Pallas kernels, shards(): pl.pallas_call(functools.partial(kernel, (ncore, nctx, ntp, rows, heads,...  81.4 us
    unnamed x1, local copies, waits for them, and re-layouts  1.98 us

profile of v1, /device:TPU:8, one launch (start us, length us, event | category | flops | bytes accessed | tf_op | source)
XLA Modules:
  0.0 83.4 jit_solution(427278680875089317)
XLA Ops:
  0.0 81.4 %attend_project.1 = bf16[1,512,640]{2,1,0:T(8,128)(2,1)} custom-call(bf16[1,512,512]{2,1,0:T(8,128)(2,1)} %q_hbm.1, bf16[1,512,128]{2,1,0:T(8,128)(2,1)} %k_hbm.1, bf16[1,512,128]{2,1,0:T(8,128)(2,1)} %v_hbm.1, s32[1,16]{1,0:T(1,128)} %lens.1, bf16[512,2560]{1,0:T(8,128)(2,1)} %w_hbm.1), custom_call_target="tpu_custom_call" | custom-call | tf_op jit(solution)/shard_map/attend_project/pallas_call | solution.py:315
  81.4 2.0 %copy.7 = bf16[1,512,640]{2,1,0:T(8,128)(2,1)} copy(bf16[1,512,640]{2,1,0:T(8,128)(2,1)} %attend_project.1) | data formatting | bytes 1310720

commit v2 on v1

v2 whole, which is shorter than its diff:
```python
import functools

import jax
import jax.numpy as jnp
from jax import lax
from jax.experimental import pallas as pl
from jax.experimental.pallas import tpu as pltpu
from jax.sharding import PartitionSpec as P

HEAD = 128
LOG2E = 1.4426950408889634
APART = 16384.0
MESH = pl.DeviceIdType.MESH


def kernel(
    shape, q_hbm, k_hbm, v_hbm, lens, w_hbm, mine_hbm, take_hbm,
    qv, kc, vc, kd, qd, qc, sc, mx, acc, att, wb, mine, give,
    loc_sem, zs, zr, xs, xr, ws, wr, fs, fr, ags, agr, fws, fwr, rss, rsr, outs,
):
    ncore, nctx, ntp, rows, heads, chunk = shape
    nchunk = rows // chunk
    half = chunk // 2
    stacked = heads * chunk
    cols = wb.shape[2] // 2
    slots = kc.shape[0]
    hops = (slots - 1) // 2
    ny = ntp // 2
    parts = zs.shape[1] // 2
    span = rows // parts
    wparts = fs.shape[1]
    wspan = rows // wparts

    core, ctx, tp = lax.axis_index("dp"), lax.axis_index("ctx"), lax.axis_index("tp")
    z, lo = ctx // 2, ctx % 2
    nz = nctx // 2
    y, hi = tp // 2, tp % 2
    up = (core, (ctx + 2) % nctx, tp)
    down = (core, (ctx + nctx - 2) % nctx, tp)
    pair = (core, ctx + 1 - 2 * lo, tp)
    yp = (core, ctx, (tp + 2) % ntp)
    ym = (core, ctx, (tp + ntp - 2) % ntp)
    yo = (core, ctx, (tp + 4) % ntp)
    mate = (core, ctx, tp + 1 - 2 * hi)
    twin = (1 - core, ctx, tp)

    barrier = pltpu.get_barrier_semaphore()
    peers = (pair, yp, ym, yo, mate, twin)

    def greet(peer):
        pl.semaphore_signal(barrier, inc=1, device_id=peer, device_id_type=MESH)

    for peer in peers:
        greet(peer)

    @pl.when(z < nz - 1)
    def _():
        greet(up)

    @pl.when(z > 0)
    def _():
        greet(down)


    def remote(src, dst, send, recv, dev):
        return pltpu.make_async_remote_copy(
            src_ref=src, dst_ref=dst, send_sem=send, recv_sem=recv, device_id=dev, device_id_type=MESH
        )

    def at_y(k):
        return lax.rem(y + k, ny)

    bank = (kc, vc)
    inputs = (k_hbm, v_hbm)

    def piece(ref, p):
        return ref.at[pl.ds((p % parts) * span, span)]

    def z_copy(j, p):
        which = bank[p // parts]
        src = inputs[p // parts].at[0] if j == 1 else which.at[2 * j - 2]
        return remote(piece(src, p), piece(which.at[2 * j], p), zs.at[j - 1, p], zr.at[j - 1, p], up)

    def x_copy(i, p, own=False):
        which = bank[p // parts]
        src = inputs[p // parts].at[0] if own else which.at[2 * i + 2 * lo]
        return remote(piece(src, p), piece(which.at[2 * i + 1], p), xs.at[i, p], xr.at[i, p], pair)

    own = [pltpu.make_async_copy(inputs[p].at[0], bank[p].at[0], loc_sem.at[p]) for p in range(2)]
    own.append(pltpu.make_async_copy(q_hbm.at[0], qv, loc_sem.at[2]))
    for c in own:
        c.start()

    has_cols = (y // 2) == core

    def w_rows(ref, r):
        return ref.at[pl.ds(r * wspan, wspan)]

    def w_copy(i, r, dst_tp):
        src = w_hbm.at[pl.ds(r * wspan, wspan), pl.ds(i * 2 * cols, 2 * cols)]
        return remote(src, w_rows(wb.at[y], r), ws.at[i, r], wr.at[y, r], (core, ctx, dst_tp))

    def w_in(g, r):
        return remote(w_rows(wb.at[g], r), w_rows(wb.at[g], r), ws.at[0, r], wr.at[g, r], yp)

    def w_here(i):
        return pltpu.make_async_copy(w_hbm.at[:, pl.ds(i * 2 * cols, 2 * cols)], wb.at[y], loc_sem.at[3])

    def w_share(g, r):
        return remote(w_rows(wb.at[g], r), w_rows(wb.at[g], r), fs.at[g, r], fr.at[g, r], twin)

    for i in range(2):

        @pl.when(2 * core + i == y)
        def _():
            w_here(i).start()

    lane = lax.broadcasted_iota(jnp.int32, (1, HEAD), 1)
    ends = jnp.zeros((1, HEAD), jnp.int32)
    starts = jnp.zeros((1, HEAD), jnp.int32)
    for j in range(lens.shape[1]):
        ends = ends + jnp.where(lane >= j, lens[0, j], 0)
        starts = starts + jnp.where(lane > j, lens[0, j], 0)
    ends = jnp.where(lane < lens.shape[1], ends, 0)

    def in_doc(first):
        pos = first + lax.broadcasted_iota(jnp.int32, (rows, HEAD), 0)
        return (pos >= starts) & (pos < ends)

    qd[...] = jnp.where(in_doc(ctx * rows), APART, 0.0).astype(jnp.bfloat16)

    def mark(d, carry):
        kd[d] = jnp.where(in_doc((ctx - d) * rows), 0.0, -1.0).astype(jnp.bfloat16)

        @pl.when(d > ctx)
        def _():
            kc[d] = jnp.zeros((rows, HEAD), jnp.bfloat16)
            vc[d] = jnp.zeros((rows, HEAD), jnp.bfloat16)

        return carry

    lax.fori_loop(0, slots, mark, 0)

    scale = LOG2E * HEAD ** (-0.5)
    dims = (((1,), (1,)), ((), ()))

    def load_queries(c):
        first = pl.multiple_of(c * chunk, chunk)
        for h in range(heads):
            qc[h * chunk : (h + 1) * chunk, 0:HEAD] = qv[pl.ds(first, chunk), h * HEAD : (h + 1) * HEAD]
            qc[h * chunk : (h + 1) * chunk, HEAD:] = qd[pl.ds(first, chunk), :]

    def score_tile(d, first):
        s = lax.dot_general(qc[...], jnp.concatenate([kc[d], kd[d]], axis=1), dims, preferred_element_type=jnp.float32)
        if d == 0:
            row = lax.broadcasted_iota(jnp.int32, (stacked, rows), 0) % chunk + first
            col = lax.broadcasted_iota(jnp.int32, (stacked, rows), 1)
            s = jnp.where(col <= row, s, -1e30)
        sc[:, d * rows : (d + 1) * rows] = s
        m = s[:, 0:HEAD]
        for g in range(1, rows // HEAD):
            m = jnp.maximum(m, s[:, g * HEAD : (g + 1) * HEAD])
        mx[...] = jnp.maximum(mx[...], m)

    ones = jnp.ones((rows, HEAD), jnp.bfloat16)

    def value_tile(d, peak):
        w16 = jnp.exp2(sc[:, d * rows : (d + 1) * rows] * scale - peak).astype(jnp.bfloat16)
        acc[...] += jnp.dot(w16, jnp.concatenate([vc[d], ones], axis=1), preferred_element_type=jnp.float32)

    for c in own:
        c.wait()
    load_queries(0)
    mx[...] = jnp.full(mx.shape, -1e30, jnp.float32)

    pl.semaphore_wait(barrier, len(peers) + jnp.where(z > 0, 1, 0) + jnp.where(z < nz - 1, 1, 0))

    def z_sends(j):
        return (z >= j - 1) & (z < nz - 1)

    def x_sends(i):
        return z >= i + lo

    def x_comes(i):
        return z >= i + 1 - lo

    for p in range(2 * parts):

        @pl.when(z_sends(1))
        def _():
            z_copy(1, p).start()

        @pl.when(lo == 0)
        def _():
            x_copy(0, p, True).start()

    for r in range(wparts):
        for i in range(2):
            dst_y = 2 * core + i

            @pl.when(dst_y != y)
            def _():
                w_copy(i, r, dst_y * 2 + hi).start()

    score_tile(0, 0)

    def weights_on(r):
        @pl.when(has_cols)
        def _():
            for k in range(1, ny):
                g = at_y(k)
                w_in(g, r).wait_recv()
                w_share(g, r).start()

    @pl.when(has_cols)
    def _():
        for i in range(2):

            @pl.when(2 * core + i == y)
            def _():
                w_here(i).wait()

        for r in range(wparts):
            w_share(y, r).start()

    for j in range(1, hops + 1):
        for p in range(2 * parts):

            @pl.when(z >= j)
            def _():
                z_copy(j, p).wait_recv()

            if j < hops:

                @pl.when(z_sends(j + 1))
                def _():
                    z_copy(j + 1, p).start()

                @pl.when(x_sends(j - lo))
                def _():
                    x_copy(j - lo, p).start()
            else:

                @pl.when((lo == 1) & x_sends(hops - 1))
                def _():
                    x_copy(hops - 1, p).start()

        score_tile(2 * j, 0)
        if j >= 2:
            for p in range(2 * parts):

                @pl.when(x_comes(j - 2))
                def _():
                    x_copy(j - 2, p).wait_recv()

            score_tile(2 * j - 3, 0)
            if j - 2 < wparts - 1:
                weights_on(j - 2)
    for p in range(2 * parts):

        @pl.when(x_comes(hops - 1))
        def _():
            x_copy(hops - 1, p).wait_recv()

    score_tile(2 * hops - 1, 0)

    def attend(c):
        acc[...] = jnp.zeros_like(acc)
        peak = jnp.max(mx[...], axis=1, keepdims=True) * scale

        @pl.when(c < nchunk - 1)
        def _():
            load_queries(c + 1)
            mx[...] = jnp.full(mx.shape, -1e30, jnp.float32)
            for d in range(slots):
                value_tile(d, peak)
                score_tile(d, (c + 1) * chunk)

        @pl.when(c == nchunk - 1)
        def _():
            for d in range(slots):
                value_tile(d, peak)

        first = pl.multiple_of(c * chunk, chunk)
        for h in range(heads):
            part = acc[h * chunk : (h + 1) * chunk, 0:HEAD] / acc[h * chunk : (h + 1) * chunk, HEAD:]
            att[y, pl.ds(first, chunk), h * HEAD : (h + 1) * HEAD] = part.astype(jnp.bfloat16)

    def spread(c, way):
        rng = pl.ds(pl.multiple_of(c * chunk, chunk), chunk)
        ref = att.at[y, rng]
        return remote(ref, ref, ags.at[way, c], agr.at[way, c], (yp, ym)[way])

    def spread_in(c, way):
        rng = pl.ds(pl.multiple_of(c * chunk, chunk), chunk)
        ref = att.at[at_y(ny - 1 if way == 0 else 1), rng]
        return remote(ref, ref, ags.at[way, c], agr.at[way, c], (yp, ym)[way])

    def pass_on(c, way):
        rng = pl.ds(pl.multiple_of(c * chunk + way * half, half), half)
        ref = att.at[at_y(ny - 1 if way == 0 else 1), rng]
        return remote(ref, ref, fws.at[way, c], fwr.at[way, c], (yp, ym)[way])

    def pass_in(c, way):
        rng = pl.ds(pl.multiple_of(c * chunk + way * half, half), half)
        ref = att.at[at_y(2), rng]
        return remote(ref, ref, fws.at[way, c], fwr.at[way, c], (yp, ym)[way])

    def swap(c):
        rng = pl.ds(pl.multiple_of(c * chunk, chunk), chunk)
        return remote(give.at[rng], take_hbm.at[rng], rss.at[c], rsr.at[c], mate)

    def to_out(c):
        rng = pl.ds(pl.multiple_of(c * chunk, chunk), chunk)
        return pltpu.make_async_copy(mine.at[rng], mine_hbm.at[rng], outs.at[c])

    def product(c, side):
        rng = pl.ds(pl.multiple_of(c * chunk, chunk), chunk)
        first = pl.multiple_of(side * cols, HEAD)
        total = jnp.dot(att[0, rng, :], wb[0, :, pl.ds(first, cols)], preferred_element_type=jnp.float32)
        for g in range(1, ny):
            total += jnp.dot(att[g, rng, :], wb[g, :, pl.ds(first, cols)], preferred_element_type=jnp.float32)
        return total

    def step(it, carry):
        @pl.when(it < nchunk)
        def _():
            attend(it)
            for way in range(2):
                spread(it, way).start()

        @pl.when(it == 0)
        def _():
            weights_on(wparts - 1)

        @pl.when((it >= 1) & (it <= nchunk))
        def _():
            for way in range(2):
                spread_in(it - 1, way).wait_recv()
                pass_on(it - 1, way).start()

        @pl.when((it == 2) & jnp.logical_not(has_cols))
        def _():
            for g in range(ny):
                for r in range(wparts):
                    w_share(g, r).wait_recv()

        @pl.when((it >= 2) & (it <= nchunk + 1))
        def _():
            c = it - 2
            rng = pl.ds(pl.multiple_of(c * chunk, chunk), chunk)
            for way in range(2):
                pass_in(c, way).wait_recv()
            give[rng, :] = product(c, 1 - hi).astype(jnp.bfloat16)
            swap(c).start()
            mine[rng, :] = product(c, hi)
            to_out(c).start()

        return carry

    lax.fori_loop(0, nchunk + 2, step, 0)

    for j in range(1, hops + 1):
        for p in range(2 * parts):

            @pl.when(z_sends(j))
            def _():
                z_copy(j, p).wait_send()

            @pl.when(x_sends(j - 1))
            def _():
                x_copy(j - 1, p).wait_send()
    for r in range(wparts):
        for i in range(2):

            @pl.when(2 * core + i != y)
            def _():
                w_copy(i, r, tp).wait_send()

    @pl.when(has_cols)
    def _():
        for g in range(ny):
            for r in range(wparts):
                w_share(g, r).wait_send()

    def drain(c, carry):
        for way in range(2):
            spread(c, way).wait_send()
            pass_on(c, way).wait_send()
        swap(c).wait()
        to_out(c).wait()
        return carry

    lax.fori_loop(0, nchunk, drain, 0)


def shards(ncore, nctx, ntp, queries, keys, values, document_lengths, out_weight):
    rows = queries.shape[1]
    heads = queries.shape[2] // keys.shape[2]
    depth = out_weight.shape[0]
    cols = out_weight.shape[1] * ncore // ntp
    chunk = 128
    nchunk = rows // chunk
    hops = 4
    slots = 2 * hops + 1
    parts, wparts = 2, 4
    ny = ntp // 2
    bf16, f32 = jnp.bfloat16, jnp.float32
    dma = pltpu.SemaphoreType.DMA
    any_spec = pl.BlockSpec(memory_space=pl.ANY)
    mine, take = pl.pallas_call(
        functools.partial(kernel, (ncore, nctx, ntp, rows, heads, chunk)),
        out_shape=(jax.ShapeDtypeStruct((rows, cols), f32), jax.ShapeDtypeStruct((rows, cols), bf16)),
        in_specs=[any_spec, any_spec, any_spec, pl.BlockSpec(memory_space=pltpu.SMEM), any_spec],
        out_specs=(any_spec, any_spec),
        scratch_shapes=[
            pltpu.VMEM((rows, heads * HEAD), bf16),
            pltpu.VMEM((slots, rows, HEAD), bf16),
            pltpu.VMEM((slots, rows, HEAD), bf16),
            pltpu.VMEM((slots, rows, HEAD), bf16),
            pltpu.VMEM((rows, HEAD), bf16),
            pltpu.VMEM((heads * chunk, 2 * HEAD), bf16),
            pltpu.VMEM((heads * chunk, slots * rows), f32),
            pltpu.VMEM((heads * chunk, HEAD), f32),
            pltpu.VMEM((heads * chunk, 2 * HEAD), f32),
            pltpu.VMEM((ny, rows, heads * HEAD), bf16),
            pltpu.VMEM((ny, depth, 2 * cols), bf16),
            pltpu.VMEM((rows, cols), f32),
            pltpu.VMEM((rows, cols), bf16),
            dma((4,)),
            dma((hops, 2 * parts)), dma((hops, 2 * parts)), dma((hops, 2 * parts)), dma((hops, 2 * parts)),
            dma((2, wparts)), dma((ny, wparts)), dma((ny, wparts)), dma((ny, wparts)),
            dma((2, nchunk)), dma((2, nchunk)), dma((2, nchunk)), dma((2, nchunk)),
            dma((nchunk,)), dma((nchunk,)), dma((nchunk,)),
        ],
        compiler_params=pltpu.CompilerParams(
            collective_id=0, has_side_effects=True, vmem_limit_bytes=56 * 1024 * 1024
        ),
        name="attend_project",
    )(queries, keys, values, document_lengths, out_weight)
    return (mine + take.astype(f32)).astype(bf16)[None]


def solution(mesh):
    sizes = (mesh.shape["dp"], mesh.shape["ctx"], mesh.shape["tp"])
    in_specs = (P("dp", "ctx", "tp"), P("dp", "ctx", "tp"), P("dp", "ctx", "tp"), P("dp", None), P("tp", "dp"))
    return jax.shard_map(
        functools.partial(shards, *sizes), mesh=mesh, in_specs=in_specs, out_specs=P("dp", "ctx", "tp"), check_vma=False
    )
```

time: 83.5 us -> 68.7 us (0.82)
  the two profiles are of different devices: /device:TPU:8 before, /device:TPU:96 now
where the time goes in v2:
time: 68.7 us; the launch traced here: 68.5 us
  Pallas kernels  66 us (96%)
  other arithmetic  2.43 us (4%)
    pallas_call x1, Pallas kernels, shards(): pl.pallas_call(functools.partial(kernel, (ncore, nctx, ntp, rows, heads,...  66 us
    broadcast_in_dim x1, other arithmetic, shards(): return (mine + take.astype(f32)).astype(bf16)[None]  2.43 us

profile of v2, /device:TPU:96, one launch (start us, length us, event | category | flops | bytes accessed | tf_op | source)
XLA Modules:
  0.0 68.5 jit_solution(116881452950026982)
XLA Ops:
  0.0 66.0 %attend_project.1 = (f32[512,640]{1,0:T(8,128)}, bf16[512,640]{1,0:T(8,128)(2,1)}) custom-call(bf16[1,512,512]{2,1,0:T(8,128)(2,1)} %q_hbm.1, bf16[1,512,128]{2,1,0:T(8,128)(2,1)} %k_hbm.1, bf16[1,512,128]{2,1,0:T(8,128)(2,1)} %v_hbm.1, s32[1,16]{1,0:T(1,128)} %lens.1, bf16[512,2560]{1,0:T(8,128)(2,1)} %w_hbm.1), custom_call_target="tpu_custom_call" | custom-call | tf_op jit(solution)/shard_map/attend_project/pallas_call | solution.py:411
  66.0 2.4 %fusion = bf16[1,512,640]{2,1,0:T(8,128)(2,1)} fusion(f32[512,640]{1,0:T(8,128)} %get-tuple-element.7, bf16[512,640]{1,0:T(8,128)(2,1)} %get-tuple-element.8), kind=kLoop, calls=%fused_computation.1 | loop fusion | flops 983040 | bytes 2621440 | tf_op jit(solution)/shard_map/broadcast_in_dim | solution.py:441

commit v3 on v2

--- a/solution.py
+++ b/solution.py
@@ -306,6 +306,12 @@
         ref = att.at[at_y(2), rng]
         return remote(ref, ref, fws.at[way, c], fwr.at[way, c], (yp, ym)[way])
 
+    last = nchunk - 1
+
+    def across(g):
+        ref = att.at[g, pl.ds(last * chunk, chunk)]
+        return remote(ref, ref, fws.at[0, last], fwr.at[0, last], yo)
+
     def swap(c):
         rng = pl.ds(pl.multiple_of(c * chunk, chunk), chunk)
         return remote(give.at[rng], take_hbm.at[rng], rss.at[c], rsr.at[c], mate)
@@ -329,6 +335,10 @@
             for way in range(2):
                 spread(it, way).start()
 
+            @pl.when(it == last)
+            def _():
+                across(y).start()
+
         @pl.when(it == 0)
         def _():
             weights_on(wparts - 1)
@@ -337,7 +347,10 @@
         def _():
             for way in range(2):
                 spread_in(it - 1, way).wait_recv()
-                pass_on(it - 1, way).start()
+
+                @pl.when(it - 1 < last)
+                def _():
+                    pass_on(it - 1, way).start()
 
         @pl.when((it == 2) & jnp.logical_not(has_cols))
         def _():
@@ -349,11 +362,19 @@
         def _():
             c = it - 2
             rng = pl.ds(pl.multiple_of(c * chunk, chunk), chunk)
-            for way in range(2):
-                pass_in(c, way).wait_recv()
+
+            @pl.when(c < last)
+            def _():
+                for way in range(2):
+                    pass_in(c, way).wait_recv()
+
+            @pl.when(c == last)
+            def _():
+                across(at_y(2)).wait_recv()
+
             give[rng, :] = product(c, 1 - hi).astype(jnp.bfloat16)
             swap(c).start()
-            mine[rng, :] = product(c, hi)
+            mine[rng, :] = product(c, hi).astype(jnp.bfloat16)
             to_out(c).start()
 
         return carry
@@ -386,12 +407,17 @@
     def drain(c, carry):
         for way in range(2):
             spread(c, way).wait_send()
-            pass_on(c, way).wait_send()
+
+            @pl.when(c < last)
+            def _():
+                pass_on(c, way).wait_send()
+
         swap(c).wait()
         to_out(c).wait()
         return carry
 
     lax.fori_loop(0, nchunk, drain, 0)
+    across(y).wait_send()
 
 
 def shards(ncore, nctx, ntp, queries, keys, values, document_lengths, out_weight):
@@ -410,7 +436,7 @@
     any_spec = pl.BlockSpec(memory_space=pl.ANY)
     mine, take = pl.pallas_call(
         functools.partial(kernel, (ncore, nctx, ntp, rows, heads, chunk)),
-        out_shape=(jax.ShapeDtypeStruct((rows, cols), f32), jax.ShapeDtypeStruct((rows, cols), bf16)),
+        out_shape=(jax.ShapeDtypeStruct((rows, cols), bf16), jax.ShapeDtypeStruct((rows, cols), bf16)),
         in_specs=[any_spec, any_spec, any_spec, pl.BlockSpec(memory_space=pltpu.SMEM), any_spec],
         out_specs=(any_spec, any_spec),
         scratch_shapes=[
@@ -425,7 +451,7 @@
             pltpu.VMEM((heads * chunk, 2 * HEAD), f32),
             pltpu.VMEM((ny, rows, heads * HEAD), bf16),
             pltpu.VMEM((ny, depth, 2 * cols), bf16),
-            pltpu.VMEM((rows, cols), f32),
+            pltpu.VMEM((rows, cols), bf16),
             pltpu.VMEM((rows, cols), bf16),
             dma((4,)),
             dma((hops, 2 * parts)), dma((hops, 2 * parts)), dma((hops, 2 * parts)), dma((hops, 2 * parts)),
@@ -438,7 +464,7 @@
         ),
         name="attend_project",
     )(queries, keys, values, document_lengths, out_weight)
-    return (mine + take.astype(f32)).astype(bf16)[None]
+    return (mine.astype(f32) + take.astype(f32)).astype(bf16)[None]
 
 
 def solution(mesh):

time: 68.7 us -> 69.7 us (1.015)
  Pallas kernels: 66 us -> 67.2 us
    pallas_call x1, Pallas kernels: 66 us -> 67.2 us  [shards(): pl.pallas_call(functools.partial(kernel, (ncore, nctx, ntp, rows, heads,...]
where the time goes in v3:
time: 69.7 us; the launch traced here: 69.5 us
  Pallas kernels  67.2 us (96%)
  other arithmetic  2.28 us (3%)
    pallas_call x1, Pallas kernels, shards(): pl.pallas_call(functools.partial(kernel, (ncore, nctx, ntp, rows, heads,...  67.2 us
    broadcast_in_dim x1, other arithmetic, shards(): return (mine.astype(f32) + take.astype(f32)).astype(bf16)[None]  2.28 us

profile of v3, /device:TPU:96, one launch (start us, length us, event | category | flops | bytes accessed | tf_op | source)
XLA Modules:
  0.0 69.5 jit_solution(17841504246486231387)
XLA Ops:
  0.0 67.2 %attend_project.1 = (bf16[512,640]{1,0:T(8,128)(2,1)}, bf16[512,640]{1,0:T(8,128)(2,1)}) custom-call(bf16[1,512,512]{2,1,0:T(8,128)(2,1)} %q_hbm.1, bf16[1,512,128]{2,1,0:T(8,128)(2,1)} %k_hbm.1, bf16[1,512,128]{2,1,0:T(8,128)(2,1)} %v_hbm.1, s32[1,16]{1,0:T(1,128)} %lens.1, bf16[512,2560]{1,0:T(8,128)(2,1)} %w_hbm.1), custom_call_target="tpu_custom_call" | custom-call | tf_op jit(solution)/shard_map/attend_project/pallas_call | solution.py:437
  67.2 2.3 %fusion = bf16[1,512,640]{2,1,0:T(8,128)(2,1)} fusion(bf16[512,640]{1,0:T(8,128)(2,1)} %get-tuple-element.8, bf16[512,640]{1,0:T(8,128)(2,1)} %get-tuple-element.7), kind=kLoop, calls=%fused_computation.1 | loop fusion | flops 1310720 | bytes 1966080 | tf_op jit(solution)/shard_map/broadcast_in_dim | solution.py:467
